TPU v7x, 32 devices: a whole 2x2x4 slice. The times are simulated.
32 devices in a mesh: section: 4 (over z), space: 8 (over y, x, core).
Axes of the slice: x: 2, y: 2, z: 4, core: 2. Of those that a mesh axis runs over, the one named last changes fastest.
Arguments:
- features: bfloat16 [4, 32, 784, 256], P('section', 'space')
- tissue: int32 [4, 32], P('section'), may hold values from 0 to 1, as said below
- first_weight: bfloat16 [256, 512], replicated, may hold values from -0.375 to 0.375
- first_gain: float32 [512], replicated, may hold values from 0.1 to 1.9
- first_bias: float32 [512], replicated, may hold values from -3 to 3
- second_weight: bfloat16 [512, 1024], P(None, 'space'), may hold values from -0.25 to 0.25
- second_gain: float32 [1024], replicated, may hold values from 0.1 to 1.9
- second_bias: float32 [1024], replicated, may hold values from -3 to 3
Outputs:
- output: bfloat16 [4, 1024, 25088], P('section', 'space')
- first_mean: float32 [512], replicated
- first_var: float32 [512], replicated
- second_mean: float32 [1024], P('space')
- second_var: float32 [1024], P('space')
Inputs may be any that keep to these rules, and one draw needn't show every extreme that they name: Every tile row holds at least one tissue tile and at least one tile without tissue.
All inputs are finite; a program needn't handle non-finite values.
Results may differ from a plain program's by a relative error of at most 0.0053.
Values may be sent and summed in bfloat16 or wider, within the bound.
A program may use at most 128 MiB of HBM per device.

v0:
```python
import jax
import jax.numpy as jnp
from jax import lax
from jax.sharding import PartitionSpec as P

EPS = 1e-05


def normalize(values, mean_val, var_val, gain, bias):
    return jnp.maximum(gain * (values - mean_val) * lax.rsqrt(var_val + EPS) + bias, 0.0)


def masked_sum(values, weight):
    return jnp.sum(values * weight, axis=(0, 1, 2))


def channel_first(values):
    batch, tiles_here, pixels, chans = values.shape
    return jnp.transpose(values, (0, 3, 1, 2)).reshape(batch, chans, tiles_here * pixels)


def shards(
    features, tissue, first_weight, first_gain, first_bias, second_weight, second_gain, second_bias
):
    index = lax.axis_index("space")
    tiles_here = features.shape[1]
    pixels = features.shape[2]
    row_mask = tissue[0].astype(jnp.float32)
    own_mask = lax.dynamic_slice_in_dim(row_mask, index * tiles_here, tiles_here)
    own_weight = own_mask[None, :, None, None]
    local_count = jnp.sum(own_mask) * pixels
    first = jnp.einsum("mtpc,cd->mtpd", features, first_weight, preferred_element_type=jnp.float32)
    total, squares, count = lax.psum(
        (
            masked_sum(first, own_weight),
            jnp.sum(first * first * own_weight, axis=(0, 1, 2)),
            local_count,
        ),
        ("section", "space"),
    )
    first_mean = total / count
    first_var = squares / count - first_mean * first_mean
    activation = normalize(first, first_mean, first_var, first_gain, first_bias).astype(
        jnp.bfloat16
    )
    second = jnp.einsum(
        "mtpc,cd->mtpd",
        activation,
        lax.all_gather(second_weight, "space", axis=1, tiled=True),
        preferred_element_type=jnp.float32,
    )
    width_here = second_weight.shape[1]
    moved = lax.all_to_all(channel_first(second), "space", split_axis=1, concat_axis=2, tiled=True)
    row_weight = jnp.repeat(row_mask, pixels)[None, None, :]
    total_two, squares_two = lax.psum(
        (
            jnp.sum(moved * row_weight, axis=(0, 2)),
            jnp.sum(moved * moved * row_weight, axis=(0, 2)),
        ),
        "section",
    )
    second_mean = total_two / count
    second_var = squares_two / count - second_mean * second_mean
    gain_here = lax.dynamic_slice_in_dim(second_gain, index * width_here, width_here)
    bias_here = lax.dynamic_slice_in_dim(second_bias, index * width_here, width_here)
    output = normalize(
        moved, second_mean[:, None], second_var[:, None], gain_here[:, None], bias_here[:, None]
    ).astype(jnp.bfloat16)
    return (output, first_mean, first_var, second_mean, second_var)


def solution(mesh):
    in_specs = (
        P("section", "space", None, None),
        P("section", None),
        P(),
        P(),
        P(),
        P(None, "space"),
        P(),
        P(),
    )
    out_specs = (P("section", "space", None), P(), P(), P("space"), P("space"))
    return jax.shard_map(shards, mesh=mesh, in_specs=in_specs, out_specs=out_specs, check_vma=False)
```

profile of v0, /device:TPU:0, one launch (start us, length us, event | category | flops | bytes accessed | tf_op | source)
XLA Modules:
  0.0 314.5 jit_solution(18157507239745372082)
XLA Ops:
  7.2 0.0 copy-start
  7.2 0.0 all-gather.2.cloned.1.call-start
  7.2 0.7 all-gather.2.cloned.1.call-update
  7.9 0.7 convert_element_type.23
  8.6 0.7 fusion.15
  9.9 0.0 copy-done
  9.9 0.0 copy-start.4
  9.9 0.0 copy-start.5
  9.9 4.9 %multiply_reduce_fusion.3 = (f32[512]{0:T(512)S(1)}, f32[512]{0:T(512)S(1)}, f32[4,784,512]{2,1,0:T(8,128)}) fusion(f32[4]{0:T(128)S(1)} %get-tuple-element.36, bf16[256,512]{1,0:T(8,128)(2,1)} %param.10, bf16[1,4,784,256]{3,2,1,0:T(8,128)(2,1)S(1)} %copy-done), kind=kOutput, calls=%fused_computation.10 | convolution fusion | flops 830110720 | bytes 8294416 | tf_op jit(solution)/shard_map/mtpc,cd->mtpd/dot_general | solution.py:32
  14.8 41.9 %all-reduce = (f32[512]{0:T(512)S(1)}, f32[512]{0:T(512)S(1)}, f32[]{:T(128)}) all-reduce(f32[512]{0:T(512)S(1)} %get-tuple-element.23, f32[512]{0:T(512)S(1)} %get-tuple-element.22, f32[]{:T(128)S(6)} %mul.118), channel_id=1, replica_groups=mesh['section'=4,'space'=8] {'section','space'}, use_global_device_ids=true, to_apply=%region_5.0 | all-reduce | flops 1025 | bytes 8200 | tf_op jit(solution)/shard_map/psum | solution.py:33
  56.8 1.2 add_rsqrt_fusion
  58.0 0.0 copy-start.3
  58.0 0.0 all-gather.2.cloned.1.call-done
  58.0 0.0 copy-done.4
  58.0 0.0 copy-done.5
  58.0 11.2 %fusion.5 = f32[4,784,1024]{2,1,0:T(8,128)} fusion(f32[4,784,512]{2,1,0:T(8,128)} %get-tuple-element.37, f32[512]{0:T(512)S(1)} %copy-done.4, f32[512]{0:T(512)S(1)} %get-tuple-element.32, f32[512]{0:T(512)S(1)} %get-tuple-element.34, f32[512]{0:T(512)S(1)} %copy-done.5, bf16[512,1024]{1,0:T(8,128)(2,1)} %all-gather.2.cloned.1.call-done), kind=kOutput, calls=%fused_computation.11 | convolution fusion | flops 3297968128 | bytes 20324352 | tf_op jit(solution)/shard_map/mtpc,cd->mtpd/dot_general | solution.py:46
  69.2 0.0 copy-done.3
  69.2 27.1 %copy.18 = f32[1,1024,3136]{2,0,1:T(1,128)} copy(f32[1,1024,3136]{1,2,0:T(8,128)} %bitcast.37) | data formatting | bytes 25690112 | tf_op jit(solution)/shard_map/reshape | solution.py:19
  96.3 0.0 copy-start.6
  96.3 5.5 %all-to-all-start = ((f32[1,1024,3136]{2,0,1:T(1,128)}), f32[1,1024,3136]{2,0,1:T(1,128)}, u32[]{:S(2)}, u32[]{:S(2)}) async-start(f32[1,1024,3136]{2,0,1:T(1,128)} %copy.18), calls=%async_computation | async-start | bytes 26214400 | tf_op jit(solution)/shard_map/all_to_all | solution.py:53
  101.8 0.0 copy-done.6
  101.9 0.1 convert_element_type.25
  102.0 0.1 broadcast_in_dim.4
  102.1 0.1 broadcast_in_dim.5
  102.2 0.8 dynamic_slice.11
  102.9 0.8 dynamic_slice.14
  103.7 142.8 %all-to-all-done = f32[1,1024,3136]{2,0,1:T(1,128)} async-done(((f32[1,1024,3136]{2,0,1:T(1,128)}), f32[1,1024,3136]{2,0,1:T(1,128)}, u32[]{:S(2)}, u32[]{:S(2)}) %all-to-all-start) | async-done | bytes 12845088 | tf_op jit(solution)/shard_map/all_to_all | solution.py:53
  246.5 10.3 %copy.21 = f32[1,1024,3136]{2,1,0:T(8,128)} copy(f32[1,1024,3136]{2,0,1:T(1,128)} %all-to-all-done) | data formatting | bytes 25690112
  256.8 13.6 %copy.19 = f32[1,128,8,3136]{1,3,2,0:T(8,128)} copy(f32[1,128,8,3136]{3,1,2,0:T(8,128)} %bitcast.35) | data formatting | bytes 25690112 | tf_op jit(solution)/shard_map/all_to_all | solution.py:53
  270.3 7.4 %multiply_reduce_fusion.1 = (f32[128]{0:T(128)S(1)}, f32[128]{0:T(128)S(1)}) fusion(f32[1,128,8,3136]{3,1,2,0:T(8,128)} %bitcast.36, f32[8,3136]{1,0:T(8,128)S(1)} %broadcast_in_dim.5), kind=kLoop, calls=%fused_computation.1 | loop fusion | flops 16056064 | bytes 12946432 | tf_op jit(solution)/shard_map/reduce_sum | solution.py:57
  277.7 10.6 %all-reduce.1 = (f32[128]{0:T(128)S(1)}, f32[128]{0:T(128)S(1)}) all-reduce(f32[128]{0:T(128)S(1)} %get-tuple-element.21, f32[128]{0:T(128)S(1)} %get-tuple-element.20), channel_id=1, replica_groups=mesh['section'=4,'space'=8] {'section'}, use_global_device_ids=true, to_apply=%region_9.0 | all-reduce | flops 256 | bytes 2048 | tf_op jit(solution)/shard_map/psum | solution.py:55
  288.4 1.2 add_rsqrt_fusion.1
  289.5 0.0 copy-start.2
  289.5 0.0 copy-start.1
  289.5 8.5 %fusion.4 = bf16[1,128,25088]{1,2,0:T(8,128)(2,1)} fusion(f32[1,128,8,3136]{1,3,2,0:T(8,128)} %copy.19, f32[128]{0:T(128)S(1)} %dynamic_slice.14, f32[128]{0:T(128)S(1)} %get-tuple-element.29, f32[128]{0:T(128)S(1)} %get-tuple-element.31, f32[128]{0:T(128)S(1)} %dynamic_slice.11), kind=kLoop, calls=%fused_computation.7 | loop fusion | flops 19267584 | bytes 19269632 | tf_op jit(solution)/shard_map/convert_element_type | solution.py:68
  298.0 0.0 copy-done.2
  298.0 9.6 %copy.20 = bf16[1,128,25088]{2,1,0:T(8,128)(2,1)} copy(bf16[1,128,25088]{1,2,0:T(8,128)(2,1)} %fusion.4) | data formatting | bytes 12845056
  307.6 0.0 copy-done.1
  (1 shorter events, 0.0 us)
Async XLA Ops:
  7.2 2.7 copy-start
  7.2 50.8 %all-gather.2.cloned.1.call-start = ((), (), s32[]{:S(2)}) async-start(), calls=%async_computation.1 | async-start | bytes 1179648 | tf_op jit(solution)/shard_map/all_gather | solution.py:49
  9.9 48.1 %copy-start.4 = (f32[512]{0:T(512)S(1)}, f32[512]{0:T(512)}, u32[]{:S(2)}) copy-start(f32[512]{0:T(512)} %param.12) | copy-start | bytes 6148
  9.9 48.1 %copy-start.5 = (f32[512]{0:T(512)S(1)}, f32[512]{0:T(512)}, u32[]{:S(2)}) copy-start(f32[512]{0:T(512)} %param.11) | copy-start | bytes 6148
  58.0 11.2 %copy-start.3 = (f32[512]{0:T(512)}, f32[512]{0:T(512)S(1)}, u32[]{:S(2)}) copy-start(f32[512]{0:T(512)S(1)} %get-tuple-element.34) | copy-start | bytes 6148
  96.3 5.5 %copy-start.6 = (s32[1,32]{1,0:T(1,128)S(1)}, s32[1,32]{1,0:T(1,128)}, u32[]{:S(2)}) copy-start(s32[1,32]{1,0:T(1,128)} %param.9) | copy-start | bytes 388
  96.3 150.2 %all-to-all-start = ((f32[1,1024,3136]{2,0,1:T(1,128)}), f32[1,1024,3136]{2,0,1:T(1,128)}, u32[]{:S(2)}, u32[]{:S(2)}) async-start(f32[1,1024,3136]{2,0,1:T(1,128)} %copy.18), calls=%async_computation | async-start | bytes 26214400 | tf_op jit(solution)/shard_map/all_to_all | solution.py:53
  289.5 8.5 %copy-start.2 = (f32[128]{0:T(128)}, f32[128]{0:T(128)S(1)}, u32[]{:S(2)}) copy-start(f32[128]{0:T(128)S(1)} %get-tuple-element.31) | copy-start | bytes 1540
  289.5 18.1 %copy-start.1 = (bf16[1,4,784,256]{3,2,1,0:T(8,128)(2,1)S(1)}, bf16[1,4,784,256]{3,2,1,0:T(8,128)(2,1)}, u32[]{:S(2)}) copy-start(bf16[1,4,784,256]{3,2,1,0:T(8,128)(2,1)} %param.8) | copy-start | bytes 4816900
Sparse Core Ops, SparseCore 0:
  9.9 26.6 all-gather.1
where the time goes:
time: 316 us; the launch traced here: 314 us
  waiting for transfers between devices  143 us (45%)
  local copies, waits for them, and re-layouts  62.4 us (20%)
  blocking collectives  52.6 us (17%)
  other arithmetic  19.6 us (6%)
  matrix products  16.1 us (5%)
  between operations  14.8 us (5%)
  starting transfers between devices  5.57 us (2%)
    all_to_all x1, waiting for transfers between devices, shards(): lax.all_to_all(channel_first(second), 'space', split_axis=1, concat_axis=...  143 us
    psum x1, blocking collectives, shards(): lax.psum((masked_sum(first, own_weight), jnp.sum(first * first * own_weig...  41.9 us
    reshape x1, local copies, waits for them, and re-layouts, channel_first(): jnp.transpose(values, (0, 3, 1, 2))  27.1 us
    unnamed x16, local copies, waits for them, and re-layouts  19.9 us
    all_to_all x1, local copies, waits for them, and re-layouts, shards(): lax.all_to_all(channel_first(second), 'space', split_axis=1, concat_axis=...  13.6 us
    dot_general x1, matrix products, shards(): jnp.einsum('mtpc,cd->mtpd', activation, lax.all_gather(second_weight, 'sp...  11.2 us
    psum x1, blocking collectives, shards(): lax.psum((jnp.sum(moved * row_weight, axis=(0, 2)), jnp.sum(moved * moved...  10.6 us
    convert_element_type x1, other arithmetic, shards(): output = normalize(moved, second_mean[:, None], second_var[:, None], gain...  8.52 us
  transfers between devices with their start and end apart: 2, of which 1 were waited for; matrix products, arithmetic and copies ran while one was open for 3% of the time, Pallas kernels for 0%

commit v1 on v0

--- a/solution.py
+++ b/solution.py
@@ -1,9 +1,14 @@
+import functools
+
 import jax
 import jax.numpy as jnp
 from jax import lax
+from jax.experimental import pallas as pl
+from jax.experimental.pallas import tpu as pltpu
 from jax.sharding import PartitionSpec as P
 
 EPS = 1e-05
+MESH = pl.DeviceIdType.MESH
 
 
 def normalize(values, mean_val, var_val, gain, bias):
@@ -19,7 +24,7 @@
     return jnp.transpose(values, (0, 3, 1, 2)).reshape(batch, chans, tiles_here * pixels)
 
 
-def shards(
+def plain_shards(
     features, tissue, first_weight, first_gain, first_bias, second_weight, second_gain, second_bias
 ):
     index = lax.axis_index("space")
@@ -69,7 +74,425 @@
     return (output, first_mean, first_var, second_mean, second_var)
 
 
+def gather_kernel(
+    shape,
+    tissue,
+    x_ref,
+    w1,
+    g1,
+    b1,
+    w2,
+    second_ref,
+    stats1_ref,
+    stats2_ref,
+    rows_all,
+    stage,
+    acc,
+    coef,
+    st1,
+    st2,
+    st3,
+    local_sem,
+    stage_sem,
+    send_a,
+    send_b,
+    send_p,
+    send_f,
+    recv_d,
+    recv_p,
+    st1_send,
+    st1_recv,
+    st2_send,
+    st2_recv,
+    st3_send,
+    st3_recv,
+):
+    n, ns, units, unit, tiles_here, pixels = shape
+    block = units * unit
+    chunk = 2 * unit
+    macros = (units + 1) // 2
+    tiles_chip = 2 * tiles_here
+    sec = lax.axis_index("section")
+    me = lax.axis_index("space")
+    core = lax.rem(me, 2)
+    cx = lax.rem(me // 2, 2)
+    cy = me // 4
+
+    def chip_at(fx, fy):
+        return lax.rem(cy + fy, 2) * 2 + lax.rem(cx + fx, 2)
+
+    chip_b = chip_at(core, 1 - core)
+    chip_a = chip_at(1 - core, core)
+    chip_d = chip_at(1, 1)
+    chip_o = chip_at(0, 0)
+    dev_a = chip_a * 2 + core
+    dev_b = chip_b * 2 + core
+    partner = chip_o * 2 + (1 - core)
+
+    def rows_of(chip, kind, k):
+        start = (chip * 2 + kind) * block + lax.rem(k + kind, units) * unit
+        return rows_all.at[pl.ds(pl.multiple_of(start, unit), unit)]
+
+    def remote(src, dst, send, recv, device):
+        return pltpu.make_async_remote_copy(
+            src_ref=src, dst_ref=dst, send_sem=send, recv_sem=recv,
+            device_id=(sec, device), device_id_type=MESH,
+        )
+
+    def own_src(k):
+        start = lax.rem(k + core, units) * unit
+        return x_ref.at[pl.ds(pl.multiple_of(start, unit), unit)]
+
+    def own_copies(k):
+        dst = rows_of(chip_o, core, k)
+        return (
+            remote(own_src(k), dst, send_a.at[k], recv_d.at[1, k], dev_a),
+            remote(own_src(k), dst, send_b.at[k], recv_d.at[0, k], dev_b),
+            remote(own_src(k), dst, send_p.at[0, k], recv_p.at[0, k], partner),
+        )
+
+    def start_own(k):
+        for copy in own_copies(k):
+            copy.start()
+
+    def relay(group, chip, k):
+        piece = rows_of(chip, core, k)
+        return remote(piece, piece, send_p.at[group, k], recv_p.at[group, k], partner)
+
+    def forward(k):
+        piece = rows_of(chip_b, core, k)
+        return remote(piece, piece, send_f.at[k], recv_d.at[2, k], dev_a)
+
+    barrier = pltpu.get_barrier_semaphore()
+    for step in range(1, n):
+        pl.semaphore_signal(
+            barrier, inc=1, device_id=(sec, lax.rem(me + step, n)), device_id_type=MESH
+        )
+    for step in range(1, ns):
+        pl.semaphore_signal(
+            barrier, inc=1, device_id=(lax.rem(sec + step, ns), me), device_id_type=MESH
+        )
+    own = pltpu.make_async_copy(
+        x_ref, rows_all.at[pl.ds(pl.multiple_of(me * block, block), block)], local_sem
+    )
+    own.start()
+    pl.semaphore_wait(barrier, n - 1 + ns - 1)
+    start_own(0)
+    own.wait()
+
+    def tile_sums(t, carry):
+        total, squares, count = carry
+        weight = tissue[0, me * tiles_here + t].astype(jnp.float32)
+        start = pl.multiple_of(me * block + t * pixels, 16)
+        first = jnp.dot(
+            rows_all[pl.ds(start, pixels), :], w1[...], preferred_element_type=jnp.float32
+        )
+        total += weight * jnp.sum(first, axis=0, keepdims=True)
+        squares += weight * jnp.sum(first * first, axis=0, keepdims=True)
+        return total, squares, count + weight * pixels
+
+    wide = w1.shape[1]
+    zero = jnp.zeros((1, wide), jnp.float32)
+    total, squares, count = lax.fori_loop(0, tiles_here, tile_sums, (zero, zero, zero))
+    mine = st1.at[me]
+    mine[0:1, :] = total
+    mine[1:2, :] = squares
+    mine[2:3, :] = count
+    mine[3:8, :] = jnp.zeros((5, wide), jnp.float32)
+
+    def exchange(buf, slot, count_of, send, recv, device_of):
+        copies = []
+        for step in range(1, count_of):
+            other = lax.rem(slot + step, count_of)
+            copy = pltpu.make_async_remote_copy(
+                src_ref=buf.at[slot], dst_ref=buf.at[slot],
+                send_sem=send.at[step], recv_sem=recv.at[slot],
+                device_id=device_of(other), device_id_type=MESH,
+            )
+            copy.start()
+            copies.append((copy, other))
+        return copies
+
+    def collect(buf, copies, recv, send, device_of):
+        for copy, other in copies:
+            copy.wait_send()
+        for step, (copy, other) in enumerate(copies):
+            pltpu.make_async_remote_copy(
+                src_ref=buf.at[other], dst_ref=buf.at[other],
+                send_sem=send.at[step + 1], recv_sem=recv.at[other],
+                device_id=device_of(other), device_id_type=MESH,
+            ).wait_recv()
+
+    def in_space(other):
+        return (sec, other)
+
+    def in_section(other):
+        return (other, me)
+
+    copies = exchange(st1, me, n, st1_send, st1_recv, in_space)
+    lax.fori_loop(1, units, lambda k, c: (start_own(k), c)[1], 0)
+    collect(st1, copies, st1_recv, st1_send, in_space)
+    st2[sec] = jnp.sum(st1[...], axis=0)
+    copies = exchange(st2, sec, ns, st2_send, st2_recv, in_section)
+    collect(st2, copies, st2_recv, st2_send, in_section)
+    sums = jnp.sum(st2[...], axis=0)
+    count = sums[2:3, :]
+    mean = sums[0:1, :] / count
+    var = sums[1:2, :] / count - mean * mean
+    scale = g1[...] * lax.rsqrt(var + EPS)
+    stats1_ref[0:1, :] = mean
+    stats1_ref[1:2, :] = var
+    stats1_ref[2:8, :] = jnp.zeros((6, wide), jnp.float32)
+    coef[0:1, :] = scale
+    coef[1:2, :] = b1[...] - mean * scale
+    coef[2:3, :] = count
+
+    acc[...] = jnp.zeros_like(acc)
+
+    def write_out(slot, start):
+        return pltpu.make_async_copy(
+            stage.at[slot], second_ref.at[:, pl.ds(start, chunk)], stage_sem.at[slot]
+        )
+
+    def compute(chip, j, slot):
+        base = chip * (2 * block) + j * chunk
+        rows = rows_all[pl.ds(pl.multiple_of(base, chunk), chunk), :]
+        first = jnp.dot(rows, w1[...], preferred_element_type=jnp.float32)
+        act = jnp.maximum(first * coef[0:1, :] + coef[1:2, :], 0.0).astype(jnp.bfloat16)
+        second = jnp.dot(act, w2[...], preferred_element_type=jnp.float32).T
+        lane = lax.broadcasted_iota(jnp.int32, (1, chunk), 1)
+        tile = (j * chunk) // pixels
+        mask = jnp.zeros((1, chunk), jnp.float32)
+        for i in range(chunk // pixels + 2):
+            at = tile + i
+            held = tissue[0, chip * tiles_chip + lax.rem(at, tiles_chip)].astype(jnp.float32)
+            low = at * pixels - j * chunk
+            mask = jnp.where((lane >= low) & (lane < low + pixels), held, mask)
+        kept = second * mask
+        square = kept * second
+        part = acc[0]
+        part2 = acc[1]
+        for i in range(chunk // 128):
+            part += kept[:, i * 128:(i + 1) * 128]
+            part2 += square[:, i * 128:(i + 1) * 128]
+        acc[0] = part
+        acc[1] = part2
+        stage[slot] = second
+        write_out(slot, pl.multiple_of(base, chunk)).start()
+
+    def compute_macro(chip, m, pending):
+        for i in range(2):
+            def go(i=i):
+                @pl.when(pending(i))
+                def _():
+                    write_out(i, 0).wait()
+                compute(chip, m + macros * i, i)
+            if i == 0:
+                go()
+            else:
+                pl.when(m < macros - 1)(go)
+
+    def incoming(kind, chip, group, k):
+        piece = rows_of(chip, kind, k)
+        if group == "relay":
+            return lambda g: remote(
+                piece, piece, send_p.at[g, k], recv_p.at[g, k], partner
+            ).wait_recv()
+        return lambda g: remote(
+            piece, piece, send_f.at[k], recv_d.at[g, k], dev_a
+        ).wait_recv()
+
+    def each_unit(m, fn):
+        fn(2 * m)
+
+        @pl.when(m < macros - 1)
+        def _():
+            fn(2 * m + 1)
+
+    def own_step(m, c):
+        each_unit(m, lambda k: incoming(1 - core, chip_o, "relay", k)(0))
+        compute_macro(chip_o, m, lambda i: m >= 1)
+        return c
+
+    def side_step(t, c):
+        s = lax.rem(t, 2)
+        m = t // 2
+        chip = chip_at(lax.rem(core + s, 2), lax.rem(1 - core + s, 2))
+        group = 1 + lax.rem(core + 1 + s, 2)
+
+        def pass_b(k):
+            incoming(core, chip_b, "direct", k)(0)
+            forward(k).start()
+            relay(2 - core, chip_b, k).start()
+
+        def pass_a(k):
+            incoming(core, chip_a, "direct", k)(1)
+            relay(1 + core, chip_a, k).start()
+
+        @pl.when(s == 0)
+        def _():
+            each_unit(m, pass_b)
+            each_unit(m, pass_a)
+
+        each_unit(m, lambda k: incoming(1 - core, chip, "relay", k)(group))
+        compute_macro(chip, m, lambda i: t >= 0)
+        return c
+
+    def last_step(m, c):
+        def pass_on(k):
+            incoming(core, chip_d, "direct", k)(2)
+            relay(3, chip_d, k).start()
+
+        each_unit(m, pass_on)
+        each_unit(m, lambda k: incoming(1 - core, chip_d, "relay", k)(3))
+        compute_macro(chip_d, m, lambda i: m >= 0)
+        return c
+
+    lax.fori_loop(0, macros, own_step, 0)
+    lax.fori_loop(0, 2 * macros, side_step, 0)
+    lax.fori_loop(0, macros, last_step, 0)
+
+    width = w2.shape[1]
+    mine = st3.at[sec]
+    mine[0:1, :] = jnp.sum(acc[0].T, axis=0, keepdims=True)
+    mine[1:2, :] = jnp.sum(acc[1].T, axis=0, keepdims=True)
+    mine[2:8, :] = jnp.zeros((6, width), jnp.float32)
+    copies = exchange(st3, sec, ns, st3_send, st3_recv, in_section)
+
+    def drain(k, c):
+        for copy in own_copies(k):
+            copy.wait_send()
+        relay(1, chip_b, k).wait_send()
+        relay(2, chip_a, k).wait_send()
+        relay(3, chip_d, k).wait_send()
+        forward(k).wait_send()
+        return c
+
+    lax.fori_loop(0, units, drain, 0)
+    for slot in range(2):
+        write_out(slot, 0).wait()
+    collect(st3, copies, st3_recv, st3_send, in_section)
+    sums = jnp.sum(st3[...], axis=0)
+    count = coef[2:3, 0:width]
+    mean = sums[0:1, :] / count
+    stats2_ref[0:1, :] = mean
+    stats2_ref[1:2, :] = sums[1:2, :] / count - mean * mean
+    stats2_ref[2:8, :] = jnp.zeros((6, width), jnp.float32)
+
+
+def finish_kernel(stats, gain, bias, second, out):
+    scale = gain[...] * lax.rsqrt(stats[1:2, :] + EPS)
+    shift = bias[...] - stats[0:1, :] * scale
+    size = scale.shape[1]
+    scale = jnp.broadcast_to(scale, (size, size)).T[:, 0:1]
+    shift = jnp.broadcast_to(shift, (size, size)).T[:, 0:1]
+    out[...] = jnp.maximum(second[...] * scale + shift, 0.0).astype(out.dtype)
+
+
+def units_of(block):
+    for units in range(3, block, 2):
+        unit = block // units
+        if block % units == 0 and unit <= 512 and unit % 64 == 0:
+            return units
+    return None
+
+
+def gather_shards(
+    n, ns, units,
+    features, tissue, first_weight, first_gain, first_bias, second_weight, second_gain, second_bias,
+):
+    index = lax.axis_index("space")
+    _, tiles_here, pixels, depth = features.shape
+    block = tiles_here * pixels
+    unit = block // units
+    wide = first_weight.shape[1]
+    width = second_weight.shape[1]
+    total = n * block
+    vmem = pl.BlockSpec(memory_space=pltpu.VMEM)
+    anyspace = pl.BlockSpec(memory_space=pl.ANY)
+    dma = pltpu.SemaphoreType.DMA
+    second, stats1, stats2 = pl.pallas_call(
+        functools.partial(gather_kernel, (n, ns, units, unit, tiles_here, pixels)),
+        out_shape=(
+            jax.ShapeDtypeStruct((width, total), jnp.float32),
+            jax.ShapeDtypeStruct((8, wide), jnp.float32),
+            jax.ShapeDtypeStruct((8, width), jnp.float32),
+        ),
+        in_specs=[pl.BlockSpec(memory_space=pltpu.SMEM), anyspace, vmem, vmem, vmem, vmem],
+        out_specs=(anyspace, vmem, vmem),
+        scratch_shapes=[
+            pltpu.VMEM((total, depth), jnp.bfloat16),
+            pltpu.VMEM((2, width, 2 * unit), jnp.float32),
+            pltpu.VMEM((2, width, 128), jnp.float32),
+            pltpu.VMEM((8, wide), jnp.float32),
+            pltpu.VMEM((n, 8, wide), jnp.float32),
+            pltpu.VMEM((ns, 8, wide), jnp.float32),
+            pltpu.VMEM((ns, 8, width), jnp.float32),
+            dma,
+            dma((2,)),
+            dma((units,)),
+            dma((units,)),
+            dma((4, units)),
+            dma((units,)),
+            dma((3, units)),
+            dma((4, units)),
+            dma((n,)),
+            dma((n,)),
+            dma((ns,)),
+            dma((ns,)),
+            dma((ns,)),
+            dma((ns,)),
+        ],
+        compiler_params=pltpu.CompilerParams(
+            collective_id=0, has_side_effects=True, vmem_limit_bytes=40 * 1024 * 1024
+        ),
+        cost_estimate=pl.CostEstimate(
+            flops=2 * total * wide * (depth + width),
+            bytes_accessed=4 * total * width + 2 * block * depth,
+            transcendentals=0,
+        ),
+        name="gather_convs",
+    )(
+        tissue,
+        features.reshape(block, depth),
+        first_weight,
+        first_gain[None, :],
+        first_bias[None, :],
+        second_weight,
+    )
+    gain_here = lax.dynamic_slice_in_dim(second_gain, index * width, width)[None, :]
+    bias_here = lax.dynamic_slice_in_dim(second_bias, index * width, width)[None, :]
+    lanes = total // 128
+    steps = next(s for s in range(7, lanes + 1) if lanes % s == 0)
+    cols = total // steps
+    output = pl.pallas_call(
+        finish_kernel,
+        out_shape=jax.ShapeDtypeStruct((width, total), jnp.bfloat16),
+        grid=(steps,),
+        in_specs=[
+            pl.BlockSpec((8, width), lambda i: (0, 0)),
+            pl.BlockSpec((1, width), lambda i: (0, 0)),
+            pl.BlockSpec((1, width), lambda i: (0, 0)),
+            pl.BlockSpec((width, cols), lambda i: (0, i)),
+        ],
+        out_specs=pl.BlockSpec((width, cols), lambda i: (0, i)),
+        compiler_params=pltpu.CompilerParams(vmem_limit_bytes=32 * 1024 * 1024),
+        name="second_norm",
+    )(stats2, gain_here, bias_here, second)
+    return output[None], stats1[0], stats1[1], stats2[0], stats2[1]
+
+
 def solution(mesh):
+    n, ns = mesh.shape["space"], mesh.shape["section"]
+
+    def shards(features, *rest):
+        block = features.shape[1] * features.shape[2]
+        units = units_of(block)
+        width = rest[4].shape[1]
+        if n == 8 and units is not None and width == 128:
+            return gather_shards(n, ns, units, features, *rest)
+        return plain_shards(features, *rest)
+
     in_specs = (
         P("section", "space", None, None),
         P("section", None),

time: 316 us -> 86.5 us (0.27)
  waiting for transfers between devices: 143 us -> 0 us
  Pallas kernels: 0 us -> 73.7 us
  blocking collectives: 52.6 us -> 0 us
  local copies, waits for them, and re-layouts: 62.4 us -> 11.8 us
  other arithmetic: 19.6 us -> 0 us
  matrix products: 16.1 us -> 0 us
  between operations: 14.8 us -> 0.66 us
  starting transfers between devices: 5.57 us -> 0 us
    all_to_all x1 -> x0, waiting for transfers between devices: 143 us -> none  [shards(): lax.all_to_all(channel_first(second), 'space', split_axis=1, concat_axis=...]
    pallas_call x0 -> x2, Pallas kernels: none -> 73.7 us  [the longest x1 68.1 us: gather_shards(): pl.pallas_call(functools.partial(gather_kernel, (n, ns, units, unit, tile...]
    psum x2 -> x0, blocking collectives: 52.6 us -> none  [the longest x1 41.9 us: shards(): lax.psum((masked_sum(first, own_weight), jnp.sum(first * first * own_weig...]
    reshape x1 -> x0, local copies, waits for them, and re-layouts: 27.1 us -> none  [channel_first(): jnp.transpose(values, (0, 3, 1, 2))]
    dot_general x2 -> x0, matrix products: 16.1 us -> none  [the longest x1 11.2 us: shards(): jnp.einsum('mtpc,cd->mtpd', activation, lax.all_gather(second_weight, 'sp...]
    all_to_all x1 -> x0, local copies, waits for them, and re-layouts: 13.6 us -> none  [shards(): lax.all_to_all(channel_first(second), 'space', split_axis=1, concat_axis=...]
    unnamed x16 -> x14, local copies, waits for them, and re-layouts: 19.9 us -> 9.93 us
    convert_element_type x3 -> x0, other arithmetic: 9.2 us -> none  [the longest x1 8.52 us: shards(): output = normalize(moved, second_mean[:, None], second_var[:, None], gain...]
  transfers between devices with their start and end apart: 2 -> 0, of which waited for: 1 -> 0; matrix products, arithmetic and copies ran while one was open for 3% -> 0% of each run, Pallas kernels for 0% -> 0%
where the time goes in v1:
time: 86.5 us; the launch traced here: 86.2 us
  Pallas kernels  73.7 us (85%)
  local copies, waits for them, and re-layouts  11.8 us (14%)
    pallas_call x1, Pallas kernels, gather_shards(): pl.pallas_call(functools.partial(gather_kernel, (n, ns, units, unit, tile...  68.1 us
    unnamed x14, local copies, waits for them, and re-layouts  9.93 us
    pallas_call x1, Pallas kernels, gather_shards(): pl.pallas_call(finish_kernel, out_shape=jax.ShapeDtypeStruct((width, tota...  5.64 us

profile of v1, /device:TPU:0, one launch (start us, length us, event | category | flops | bytes accessed | tf_op | source)
XLA Modules:
  0.0 86.2 jit_solution(10114210063553350638)
XLA Ops:
  0.6 0.8 dynamic-slice_bitcast_fusion
  1.4 0.0 copy-start.1
  1.4 1.4 %copy-done.1 = bf16[1,4,784,256]{3,2,1,0:T(8,128)(2,1)S(1)} copy-done((bf16[1,4,784,256]{3,2,1,0:T(8,128)(2,1)S(1)}, bf16[1,4,784,256]{3,2,1,0:T(8,128)(2,1)}, u32[]{:S(2)}) %copy-start.1) | copy-done | bytes 1605656
  2.8 0.0 copy-start.2
  2.8 0.9 %copy-done.2 = bf16[256,512]{1,0:T(8,128)(2,1)S(1)} copy-done((bf16[256,512]{1,0:T(8,128)(2,1)S(1)}, bf16[256,512]{1,0:T(8,128)(2,1)}, u32[]{:S(2)}) %copy-start.2) | copy-done | bytes 262168
  3.8 0.0 copy-start.3
  3.8 0.9 %copy-done.3 = bf16[512,128]{1,0:T(8,128)(2,1)S(1)} copy-done((bf16[512,128]{1,0:T(8,128)(2,1)S(1)}, bf16[512,128]{1,0:T(8,128)(2,1)}, u32[]{:S(2)}) %copy-start.3) | copy-done | bytes 131096
  4.7 0.0 copy-start.4
  4.7 0.7 copy-done.4
  5.4 0.0 copy-start.5
  5.4 0.7 copy-done.5
  6.1 0.0 copy-start.6
  6.1 0.7 copy-done.6
  6.7 68.1 %gather_convs.1 = (f32[128,25088]{1,0:T(8,128)}, f32[8,512]{1,0:T(8,128)S(1)}, f32[8,128]{1,0:T(8,128)S(1)}) custom-call(s32[1,32]{1,0:T(1,128)S(1)} %copy-done.6, bf16[3136,256]{1,0:T(8,128)(2,1)S(1)} %bitcast.14, bf16[256,512]{1,0:T(8,128)(2,1)S(1)} %copy-done.2, f32[1,512]{1,0:T(1,128)S(1)} %bitcast.15, f32[1,512]{1,0:T(1,128)S(1)} %bitcast.16, ...), custom_call_target="tpu_custom_call" | custom-call | flops 9865003008 | bytes 14450688 | tf_op jit(solution)/shard_map/gather_convs/pallas_call | solution.py:414
  74.8 0.0 copy-start
  74.8 4.6 %copy-done = f32[128,25088]{1,0:T(8,128)S(1)} copy-done((f32[128,25088]{1,0:T(8,128)S(1)}, f32[128,25088]{1,0:T(8,128)}, u32[]{:S(2)}) %copy-start) | copy-done | bytes 12845080
  79.4 5.6 %second_norm.1 = bf16[128,25088]{1,0:T(8,128)(2,1)} custom-call(f32[8,128]{1,0:T(8,128)S(1)} %get-tuple-element.8.stats, f32[1,128]{1,0:T(1,128)S(1)} %get-tuple-element.16.gain, f32[1,128]{1,0:T(1,128)S(1)} %get-tuple-element.15.bias, f32[128,25088]{1,0:T(8,128)S(1)} %copy-done), custom_call_target="tpu_custom_call" | custom-call | tf_op jit(solution)/shard_map/second_norm/pallas_call | solution.py:468
  85.1 0.5 slice_bitcast_fusion
  85.6 0.6 fusion
Async XLA Ops:
  1.4 1.4 %copy-start.1 = (bf16[1,4,784,256]{3,2,1,0:T(8,128)(2,1)S(1)}, bf16[1,4,784,256]{3,2,1,0:T(8,128)(2,1)}, u32[]{:S(2)}) copy-start(bf16[1,4,784,256]{3,2,1,0:T(8,128)(2,1)} %param.8) | copy-start | bytes 4816900
  2.8 0.9 %copy-start.2 = (bf16[256,512]{1,0:T(8,128)(2,1)S(1)}, bf16[256,512]{1,0:T(8,128)(2,1)}, u32[]{:S(2)}) copy-start(bf16[256,512]{1,0:T(8,128)(2,1)} %w1.1) | copy-start | bytes 786436
  3.8 0.9 %copy-start.3 = (bf16[512,128]{1,0:T(8,128)(2,1)S(1)}, bf16[512,128]{1,0:T(8,128)(2,1)}, u32[]{:S(2)}) copy-start(bf16[512,128]{1,0:T(8,128)(2,1)} %w2.1) | copy-start | bytes 393220
  4.7 0.7 copy-start.4
  5.4 0.7 copy-start.5
  6.1 0.7 copy-start.6
  74.8 4.7 %copy-start = (f32[128,25088]{1,0:T(8,128)S(1)}, f32[128,25088]{1,0:T(8,128)}, u32[]{:S(2)}) copy-start(f32[128,25088]{1,0:T(8,128)} %get-tuple-element.9.second) | copy-start | bytes 38535172

commit v2 on v1

--- a/solution.py
+++ b/solution.py
@@ -9,6 +9,7 @@
 
 EPS = 1e-05
 MESH = pl.DeviceIdType.MESH
+VMEM_ASKED = 32 * 1024 * 1024
 
 
 def normalize(values, mean_val, var_val, gain, bias):
@@ -76,24 +77,31 @@
 
 def gather_kernel(
     shape,
+    tissue_in,
+    x_ref,
+    w1_in,
+    g1_in,
+    b1_in,
+    w2_in,
+    g2_in,
+    b2_in,
+    second_ref,
+    stats1_ref,
+    stats2_ref,
     tissue,
-    x_ref,
     w1,
     g1,
     b1,
     w2,
-    second_ref,
-    stats1_ref,
-    stats2_ref,
+    g2,
+    b2,
     rows_all,
-    stage,
     acc,
     coef,
     st1,
     st2,
     st3,
     local_sem,
-    stage_sem,
     send_a,
     send_b,
     send_p,
@@ -172,13 +180,20 @@
         pl.semaphore_signal(
             barrier, inc=1, device_id=(lax.rem(sec + step, ns), me), device_id_type=MESH
         )
-    own = pltpu.make_async_copy(
-        x_ref, rows_all.at[pl.ds(pl.multiple_of(me * block, block), block)], local_sem
-    )
-    own.start()
+    own_rows = rows_all.at[pl.ds(pl.multiple_of(me * block, block), block)]
+    pairs = (
+        (tissue_in, tissue), (w1_in, w1), (x_ref, own_rows), (g1_in, g1), (b1_in, b1),
+        (w2_in, w2), (g2_in, g2), (b2_in, b2),
+    )
+    fetches = [
+        pltpu.make_async_copy(src, dst, local_sem.at[i]) for i, (src, dst) in enumerate(pairs)
+    ]
+    for fetch in fetches:
+        fetch.start()
     pl.semaphore_wait(barrier, n - 1 + ns - 1)
     start_own(0)
-    own.wait()
+    for fetch in fetches:
+        fetch.wait()
 
     def tile_sums(t, carry):
         total, squares, count = carry
@@ -249,12 +264,7 @@
 
     acc[...] = jnp.zeros_like(acc)
 
-    def write_out(slot, start):
-        return pltpu.make_async_copy(
-            stage.at[slot], second_ref.at[:, pl.ds(start, chunk)], stage_sem.at[slot]
-        )
-
-    def compute(chip, j, slot):
+    def compute(chip, j):
         base = chip * (2 * block) + j * chunk
         rows = rows_all[pl.ds(pl.multiple_of(base, chunk), chunk), :]
         first = jnp.dot(rows, w1[...], preferred_element_type=jnp.float32)
@@ -277,20 +287,14 @@
             part2 += square[:, i * 128:(i + 1) * 128]
         acc[0] = part
         acc[1] = part2
-        stage[slot] = second
-        write_out(slot, pl.multiple_of(base, chunk)).start()
-
-    def compute_macro(chip, m, pending):
-        for i in range(2):
-            def go(i=i):
-                @pl.when(pending(i))
-                def _():
-                    write_out(i, 0).wait()
-                compute(chip, m + macros * i, i)
-            if i == 0:
-                go()
-            else:
-                pl.when(m < macros - 1)(go)
+        second_ref[:, pl.ds(pl.multiple_of(base, chunk), chunk)] = second
+
+    def compute_macro(chip, m):
+        compute(chip, m)
+
+        @pl.when(m < macros - 1)
+        def _():
+            compute(chip, m + macros)
 
     def incoming(kind, chip, group, k):
         piece = rows_of(chip, kind, k)
@@ -311,7 +315,7 @@
 
     def own_step(m, c):
         each_unit(m, lambda k: incoming(1 - core, chip_o, "relay", k)(0))
-        compute_macro(chip_o, m, lambda i: m >= 1)
+        compute_macro(chip_o, m)
         return c
 
     def side_step(t, c):
@@ -335,7 +339,7 @@
             each_unit(m, pass_a)
 
         each_unit(m, lambda k: incoming(1 - core, chip, "relay", k)(group))
-        compute_macro(chip, m, lambda i: t >= 0)
+        compute_macro(chip, m)
         return c
 
     def last_step(m, c):
@@ -345,7 +349,7 @@
 
         each_unit(m, pass_on)
         each_unit(m, lambda k: incoming(1 - core, chip_d, "relay", k)(3))
-        compute_macro(chip_d, m, lambda i: m >= 0)
+        compute_macro(chip_d, m)
         return c
 
     lax.fori_loop(0, macros, own_step, 0)
@@ -369,24 +373,30 @@
         return c
 
     lax.fori_loop(0, units, drain, 0)
-    for slot in range(2):
-        write_out(slot, 0).wait()
     collect(st3, copies, st3_recv, st3_send, in_section)
     sums = jnp.sum(st3[...], axis=0)
     count = coef[2:3, 0:width]
     mean = sums[0:1, :] / count
+    var = sums[1:2, :] / count - mean * mean
+    scale = g2[pl.ds(me, 1), :] * lax.rsqrt(var + EPS)
     stats2_ref[0:1, :] = mean
-    stats2_ref[1:2, :] = sums[1:2, :] / count - mean * mean
-    stats2_ref[2:8, :] = jnp.zeros((6, width), jnp.float32)
-
-
-def finish_kernel(stats, gain, bias, second, out):
-    scale = gain[...] * lax.rsqrt(stats[1:2, :] + EPS)
-    shift = bias[...] - stats[0:1, :] * scale
-    size = scale.shape[1]
-    scale = jnp.broadcast_to(scale, (size, size)).T[:, 0:1]
-    shift = jnp.broadcast_to(shift, (size, size)).T[:, 0:1]
-    out[...] = jnp.maximum(second[...] * scale + shift, 0.0).astype(out.dtype)
+    stats2_ref[1:2, :] = var
+    stats2_ref[2:3, :] = scale
+    stats2_ref[3:4, :] = b2[pl.ds(me, 1), :] - mean * scale
+    stats2_ref[4:8, :] = jnp.zeros((4, width), jnp.float32)
+
+
+def finish_kernel(cols, stats1, stats2, second, out, mean1, var1, mean2, var2):
+    size = stats2.shape[1]
+    scale = jnp.broadcast_to(stats2[2:3, :], (size, size)).T[:, 0:1]
+    shift = jnp.broadcast_to(stats2[3:4, :], (size, size)).T[:, 0:1]
+    start = pl.multiple_of(pl.program_id(0) * cols, cols)
+    values = second[:, pl.ds(start, cols)]
+    out[...] = jnp.maximum(values * scale + shift, 0.0).astype(out.dtype)
+    mean1[...] = stats1[0:1, :]
+    var1[...] = stats1[1:2, :]
+    mean2[...] = stats2[0:1, :]
+    var2[...] = stats2[1:2, :]
 
 
 def units_of(block):
@@ -401,7 +411,6 @@
     n, ns, units,
     features, tissue, first_weight, first_gain, first_bias, second_weight, second_gain, second_bias,
 ):
-    index = lax.axis_index("space")
     _, tiles_here, pixels, depth = features.shape
     block = tiles_here * pixels
     unit = block // units
@@ -409,27 +418,32 @@
     width = second_weight.shape[1]
     total = n * block
     vmem = pl.BlockSpec(memory_space=pltpu.VMEM)
-    anyspace = pl.BlockSpec(memory_space=pl.ANY)
+    hbm = pl.BlockSpec(memory_space=pltpu.HBM)
     dma = pltpu.SemaphoreType.DMA
     second, stats1, stats2 = pl.pallas_call(
         functools.partial(gather_kernel, (n, ns, units, unit, tiles_here, pixels)),
         out_shape=(
-            jax.ShapeDtypeStruct((width, total), jnp.float32),
-            jax.ShapeDtypeStruct((8, wide), jnp.float32),
-            jax.ShapeDtypeStruct((8, width), jnp.float32),
-        ),
-        in_specs=[pl.BlockSpec(memory_space=pltpu.SMEM), anyspace, vmem, vmem, vmem, vmem],
-        out_specs=(anyspace, vmem, vmem),
+            pltpu.VMEM((width, total), jnp.float32),
+            pltpu.VMEM((8, wide), jnp.float32),
+            pltpu.VMEM((8, width), jnp.float32),
+        ),
+        in_specs=[hbm] * 8,
+        out_specs=(vmem, vmem, vmem),
         scratch_shapes=[
+            pltpu.SMEM(tissue.shape, jnp.int32),
+            pltpu.VMEM((depth, wide), jnp.bfloat16),
+            pltpu.VMEM((1, wide), jnp.float32),
+            pltpu.VMEM((1, wide), jnp.float32),
+            pltpu.VMEM((wide, width), jnp.bfloat16),
+            pltpu.VMEM((n, width), jnp.float32),
+            pltpu.VMEM((n, width), jnp.float32),
             pltpu.VMEM((total, depth), jnp.bfloat16),
-            pltpu.VMEM((2, width, 2 * unit), jnp.float32),
             pltpu.VMEM((2, width, 128), jnp.float32),
             pltpu.VMEM((8, wide), jnp.float32),
             pltpu.VMEM((n, 8, wide), jnp.float32),
             pltpu.VMEM((ns, 8, wide), jnp.float32),
             pltpu.VMEM((ns, 8, width), jnp.float32),
-            dma,
-            dma((2,)),
+            dma((8,)),
             dma((units,)),
             dma((units,)),
             dma((4, units)),
@@ -444,42 +458,54 @@
             dma((ns,)),
         ],
         compiler_params=pltpu.CompilerParams(
-            collective_id=0, has_side_effects=True, vmem_limit_bytes=40 * 1024 * 1024
+            collective_id=0, has_side_effects=True, vmem_limit_bytes=VMEM_ASKED
         ),
         cost_estimate=pl.CostEstimate(
             flops=2 * total * wide * (depth + width),
-            bytes_accessed=4 * total * width + 2 * block * depth,
+            bytes_accessed=2 * block * depth,
             transcendentals=0,
         ),
         name="gather_convs",
     )(
-        tissue,
-        features.reshape(block, depth),
-        first_weight,
-        first_gain[None, :],
-        first_bias[None, :],
-        second_weight,
-    )
-    gain_here = lax.dynamic_slice_in_dim(second_gain, index * width, width)[None, :]
-    bias_here = lax.dynamic_slice_in_dim(second_bias, index * width, width)[None, :]
+        *(
+            pltpu.with_memory_space_constraint(array, pltpu.HBM)
+            for array in (
+                tissue,
+                features.reshape(block, depth),
+                first_weight,
+                first_gain[None, :],
+                first_bias[None, :],
+                second_weight,
+                second_gain.reshape(n, width),
+                second_bias.reshape(n, width),
+            )
+        )
+    )
     lanes = total // 128
     steps = next(s for s in range(7, lanes + 1) if lanes % s == 0)
     cols = total // steps
-    output = pl.pallas_call(
-        finish_kernel,
-        out_shape=jax.ShapeDtypeStruct((width, total), jnp.bfloat16),
+    output, mean1, var1, mean2, var2 = pl.pallas_call(
+        functools.partial(finish_kernel, cols),
+        out_shape=(
+            jax.ShapeDtypeStruct((width, total), jnp.bfloat16),
+            jax.ShapeDtypeStruct((1, wide), jnp.float32),
+            jax.ShapeDtypeStruct((1, wide), jnp.float32),
+            jax.ShapeDtypeStruct((1, width), jnp.float32),
+            jax.ShapeDtypeStruct((1, width), jnp.float32),
+        ),
         grid=(steps,),
-        in_specs=[
-            pl.BlockSpec((8, width), lambda i: (0, 0)),
+        in_specs=[vmem, vmem, vmem],
+        out_specs=(
+            pl.BlockSpec((width, cols), lambda i: (0, i)),
+            pl.BlockSpec((1, wide), lambda i: (0, 0)),
+            pl.BlockSpec((1, wide), lambda i: (0, 0)),
             pl.BlockSpec((1, width), lambda i: (0, 0)),
             pl.BlockSpec((1, width), lambda i: (0, 0)),
-            pl.BlockSpec((width, cols), lambda i: (0, i)),
-        ],
-        out_specs=pl.BlockSpec((width, cols), lambda i: (0, i)),
-        compiler_params=pltpu.CompilerParams(vmem_limit_bytes=32 * 1024 * 1024),
+        ),
+        compiler_params=pltpu.CompilerParams(vmem_limit_bytes=VMEM_ASKED // 2),
         name="second_norm",
-    )(stats2, gain_here, bias_here, second)
-    return output[None], stats1[0], stats1[1], stats2[0], stats2[1]
+    )(*(pltpu.with_memory_space_constraint(x, pltpu.VMEM) for x in (stats1, stats2, second)))
+    return output[None], mean1[0], var1[0], mean2[0], var2[0]
 
 
 def solution(mesh):

time: 86.5 us -> 73.7 us (0.85)
  local copies, waits for them, and re-layouts: 11.8 us -> 0 us
    unnamed x14 -> x0, local copies, waits for them, and re-layouts: 9.93 us -> none
where the time goes in v2:
time: 73.7 us; the launch traced here: 73.6 us
  Pallas kernels  73 us (99%)
    pallas_call x1, Pallas kernels, gather_shards(): pl.pallas_call(functools.partial(gather_kernel, (n, ns, units, unit, tile...  67.8 us
    pallas_call x1, Pallas kernels, gather_shards(): pl.pallas_call(functools.partial(finish_kernel, cols), out_shape=(jax.Sha...  5.14 us

profile of v2, /device:TPU:0, one launch (start us, length us, event | category | flops | bytes accessed | tf_op | source)
XLA Modules:
  0.0 73.6 jit_solution(12556382617743068020)
XLA Ops:
  0.6 67.8 %gather_convs.1 = (f32[128,25088]{1,0:T(8,128)S(1)}, f32[8,512]{1,0:T(8,128)S(1)}, f32[8,128]{1,0:T(8,128)S(1)}) custom-call(s32[1,32]{1,0:T(1,128)} %tissue_in.1, bf16[3136,256]{1,0:T(8,128)(2,1)} %bitcast.11, bf16[256,512]{1,0:T(8,128)(2,1)} %w1_in.1, f32[1,512]{1,0:T(1,128)} %bitcast.14, f32[1,512]{1,0:T(1,128)} %bitcast.15, bf16[512,128]{1,0:T(8,128)(2,1)} %w2_in.1, ...), custom_call_target="tpu_custom_call" | custom-call | flops 9865003008 | bytes 1605632 | tf_op jit(solution)/shard_map/gather_convs/pallas_call | solution.py:423
  68.5 5.1 %second_norm.1 = (bf16[128,25088]{1,0:T(8,128)(2,1)}, f32[1,512]{1,0:T(1,128)}, f32[1,512]{1,0:T(1,128)}, f32[1,128]{1,0:T(1,128)}, f32[1,128]{1,0:T(1,128)}) custom-call(f32[8,512]{1,0:T(8,128)S(1)} %get-tuple-element.13.stats1, f32[8,128]{1,0:T(8,128)S(1)} %get-tuple-element.14.stats2, f32[128,25088]{1,0:T(8,128)S(1)} %get-tuple-element.15.second), custom_call_target="tpu_custom_call" | custom-call | tf_op jit(solution)/shard_map/second_norm/pallas_call | solution.py:487

commit v3 on v2

--- a/solution.py
+++ b/solution.py
@@ -9,7 +9,7 @@
 
 EPS = 1e-05
 MESH = pl.DeviceIdType.MESH
-VMEM_ASKED = 32 * 1024 * 1024
+VMEM_ASKED = 40 * 1024 * 1024
 
 
 def normalize(values, mean_val, var_val, gain, bias):
@@ -96,6 +96,7 @@
     g2,
     b2,
     rows_all,
+    acts,
     acc,
     coef,
     st1,
@@ -137,9 +138,16 @@
     dev_b = chip_b * 2 + core
     partner = chip_o * 2 + (1 - core)
 
-    def rows_of(chip, kind, k):
-        start = (chip * 2 + kind) * block + lax.rem(k + kind, units) * unit
+    def local_row(kind, k):
+        return lax.rem(k + kind, units) * unit
+
+    def rows_of(chip, k):
+        start = chip * block + local_row(core, k)
         return rows_all.at[pl.ds(pl.multiple_of(start, unit), unit)]
+
+    def acts_of(chip, kind, k):
+        start = (chip * 2 + kind) * block + local_row(kind, k)
+        return acts.at[pl.ds(pl.multiple_of(start, unit), unit)]
 
     def remote(src, dst, send, recv, device):
         return pltpu.make_async_remote_copy(
@@ -147,29 +155,29 @@
             device_id=(sec, device), device_id_type=MESH,
         )
 
-    def own_src(k):
-        start = lax.rem(k + core, units) * unit
-        return x_ref.at[pl.ds(pl.multiple_of(start, unit), unit)]
-
     def own_copies(k):
-        dst = rows_of(chip_o, core, k)
+        src = x_ref.at[pl.ds(pl.multiple_of(local_row(core, k), unit), unit)]
+        dst = rows_of(chip_o, k)
         return (
-            remote(own_src(k), dst, send_a.at[k], recv_d.at[1, k], dev_a),
-            remote(own_src(k), dst, send_b.at[k], recv_d.at[0, k], dev_b),
-            remote(own_src(k), dst, send_p.at[0, k], recv_p.at[0, k], partner),
+            remote(src, dst, send_a.at[k], recv_d.at[1, k], dev_a),
+            remote(src, dst, send_b.at[k], recv_d.at[0, k], dev_b),
         )
 
     def start_own(k):
         for copy in own_copies(k):
             copy.start()
 
-    def relay(group, chip, k):
-        piece = rows_of(chip, core, k)
+    def relay(group, chip, kind, k):
+        piece = acts_of(chip, kind, k)
         return remote(piece, piece, send_p.at[group, k], recv_p.at[group, k], partner)
 
     def forward(k):
-        piece = rows_of(chip_b, core, k)
+        piece = rows_of(chip_b, k)
         return remote(piece, piece, send_f.at[k], recv_d.at[2, k], dev_a)
+
+    def arrived(source, chip, k):
+        piece = rows_of(chip, k)
+        remote(piece, piece, send_f.at[k], recv_d.at[source, k], dev_a).wait_recv()
 
     barrier = pltpu.get_barrier_semaphore()
     for step in range(1, n):
@@ -180,7 +188,7 @@
         pl.semaphore_signal(
             barrier, inc=1, device_id=(lax.rem(sec + step, ns), me), device_id_type=MESH
         )
-    own_rows = rows_all.at[pl.ds(pl.multiple_of(me * block, block), block)]
+    own_rows = rows_all.at[pl.ds(pl.multiple_of(chip_o * block, block), block)]
     pairs = (
         (tissue_in, tissue), (w1_in, w1), (x_ref, own_rows), (g1_in, g1), (b1_in, b1),
         (w2_in, w2), (g2_in, g2), (b2_in, b2),
@@ -192,13 +200,14 @@
         fetch.start()
     pl.semaphore_wait(barrier, n - 1 + ns - 1)
     start_own(0)
+    start_own(1)
     for fetch in fetches:
         fetch.wait()
 
     def tile_sums(t, carry):
         total, squares, count = carry
         weight = tissue[0, me * tiles_here + t].astype(jnp.float32)
-        start = pl.multiple_of(me * block + t * pixels, 16)
+        start = pl.multiple_of(chip_o * block + t * pixels, 16)
         first = jnp.dot(
             rows_all[pl.ds(start, pixels), :], w1[...], preferred_element_type=jnp.float32
         )
@@ -245,7 +254,7 @@
         return (other, me)
 
     copies = exchange(st1, me, n, st1_send, st1_recv, in_space)
-    lax.fori_loop(1, units, lambda k, c: (start_own(k), c)[1], 0)
+    lax.fori_loop(2, units, lambda k, c: (start_own(k), c)[1], 0)
     collect(st1, copies, st1_recv, st1_send, in_space)
     st2[sec] = jnp.sum(st1[...], axis=0)
     copies = exchange(st2, sec, ns, st2_send, st2_recv, in_section)
@@ -264,11 +273,16 @@
 
     acc[...] = jnp.zeros_like(acc)
 
+    def activate(group, chip, k):
+        rows = rows_of(chip, k)[...]
+        first = jnp.dot(rows, w1[...], preferred_element_type=jnp.float32)
+        act = jnp.maximum(first * coef[0:1, :] + coef[1:2, :], 0.0)
+        acts_of(chip, core, k)[...] = act.astype(jnp.bfloat16)
+        relay(group, chip, core, k).start()
+
     def compute(chip, j):
         base = chip * (2 * block) + j * chunk
-        rows = rows_all[pl.ds(pl.multiple_of(base, chunk), chunk), :]
-        first = jnp.dot(rows, w1[...], preferred_element_type=jnp.float32)
-        act = jnp.maximum(first * coef[0:1, :] + coef[1:2, :], 0.0).astype(jnp.bfloat16)
+        act = acts[pl.ds(pl.multiple_of(base, chunk), chunk), :]
         second = jnp.dot(act, w2[...], preferred_element_type=jnp.float32).T
         lane = lax.broadcasted_iota(jnp.int32, (1, chunk), 1)
         tile = (j * chunk) // pixels
@@ -289,23 +303,6 @@
         acc[1] = part2
         second_ref[:, pl.ds(pl.multiple_of(base, chunk), chunk)] = second
 
-    def compute_macro(chip, m):
-        compute(chip, m)
-
-        @pl.when(m < macros - 1)
-        def _():
-            compute(chip, m + macros)
-
-    def incoming(kind, chip, group, k):
-        piece = rows_of(chip, kind, k)
-        if group == "relay":
-            return lambda g: remote(
-                piece, piece, send_p.at[g, k], recv_p.at[g, k], partner
-            ).wait_recv()
-        return lambda g: remote(
-            piece, piece, send_f.at[k], recv_d.at[g, k], dev_a
-        ).wait_recv()
-
     def each_unit(m, fn):
         fn(2 * m)
 
@@ -313,48 +310,85 @@
         def _():
             fn(2 * m + 1)
 
+    def finish(group, chip, m):
+        each_unit(m, lambda k: relay(group, chip, 1 - core, k).wait_recv())
+        compute(chip, m)
+
+        @pl.when(m < macros - 1)
+        def _():
+            compute(chip, m + macros)
+
+    def side(s):
+        chip = chip_at(lax.rem(core + s, 2), lax.rem(1 - core + s, 2))
+        return 1 + lax.rem(core + 1 + s, 2), chip
+
+    def finish_sides(m):
+        def one(s, c):
+            finish(*side(s), m)
+            return c
+
+        lax.fori_loop(0, 2, one, 0)
+
+    last = macros - 1
+
     def own_step(m, c):
-        each_unit(m, lambda k: incoming(1 - core, chip_o, "relay", k)(0))
-        compute_macro(chip_o, m)
+        each_unit(m, lambda k: activate(0, chip_o, k))
+
+        @pl.when(m > 0)
+        def _():
+            finish(0, chip_o, m - 1)
+
         return c
 
-    def side_step(t, c):
-        s = lax.rem(t, 2)
-        m = t // 2
-        chip = chip_at(lax.rem(core + s, 2), lax.rem(1 - core + s, 2))
-        group = 1 + lax.rem(core + 1 + s, 2)
-
-        def pass_b(k):
-            incoming(core, chip_b, "direct", k)(0)
+    def side_step(m, c):
+        def from_b(k):
+            arrived(0, chip_b, k)
             forward(k).start()
-            relay(2 - core, chip_b, k).start()
-
-        def pass_a(k):
-            incoming(core, chip_a, "direct", k)(1)
-            relay(1 + core, chip_a, k).start()
-
-        @pl.when(s == 0)
-        def _():
-            each_unit(m, pass_b)
-            each_unit(m, pass_a)
-
-        each_unit(m, lambda k: incoming(1 - core, chip, "relay", k)(group))
-        compute_macro(chip, m)
+
+        def from_a(k):
+            arrived(1, chip_a, k)
+
+        each_unit(m, from_b)
+        each_unit(m, from_a)
+
+        def one(s, c):
+            group, chip = side(s)
+            each_unit(m, lambda k: activate(group, chip, k))
+            return c
+
+        lax.fori_loop(0, 2, one, 0)
+
+        @pl.when(m == 0)
+        def _():
+            finish(0, chip_o, last)
+
+        @pl.when(m > 0)
+        def _():
+            finish_sides(m - 1)
+
         return c
 
     def last_step(m, c):
-        def pass_on(k):
-            incoming(core, chip_d, "direct", k)(2)
-            relay(3, chip_d, k).start()
-
-        each_unit(m, pass_on)
-        each_unit(m, lambda k: incoming(1 - core, chip_d, "relay", k)(3))
-        compute_macro(chip_d, m)
+        def from_d(k):
+            arrived(2, chip_d, k)
+            activate(3, chip_d, k)
+
+        @pl.when(m == 0)
+        def _():
+            finish_sides(last)
+
+        each_unit(m, from_d)
+
+        @pl.when(m > 0)
+        def _():
+            finish(3, chip_d, m - 1)
+
         return c
 
     lax.fori_loop(0, macros, own_step, 0)
-    lax.fori_loop(0, 2 * macros, side_step, 0)
+    lax.fori_loop(0, macros, side_step, 0)
     lax.fori_loop(0, macros, last_step, 0)
+    finish(3, chip_d, last)
 
     width = w2.shape[1]
     mine = st3.at[sec]
@@ -366,9 +400,8 @@
     def drain(k, c):
         for copy in own_copies(k):
             copy.wait_send()
-        relay(1, chip_b, k).wait_send()
-        relay(2, chip_a, k).wait_send()
-        relay(3, chip_d, k).wait_send()
+        for group in range(4):
+            relay(group, chip_o, core, k).wait_send()
         forward(k).wait_send()
         return c
 
@@ -386,17 +419,29 @@
     stats2_ref[4:8, :] = jnp.zeros((4, width), jnp.float32)
 
 
-def finish_kernel(cols, stats1, stats2, second, out, mean1, var1, mean2, var2):
+def finish_kernel(cols, stats1, stats2, second, out, mean1, var1, mean2, var2, held, sems):
     size = stats2.shape[1]
     scale = jnp.broadcast_to(stats2[2:3, :], (size, size)).T[:, 0:1]
     shift = jnp.broadcast_to(stats2[3:4, :], (size, size)).T[:, 0:1]
-    start = pl.multiple_of(pl.program_id(0) * cols, cols)
-    values = second[:, pl.ds(start, cols)]
-    out[...] = jnp.maximum(values * scale + shift, 0.0).astype(out.dtype)
+
+    def write(i):
+        span = pl.ds(pl.multiple_of(i * cols, cols), cols)
+        return pltpu.make_async_copy(held.at[:, span], out.at[:, span], sems.at[i])
+
+    def one(i, c):
+        span = pl.ds(pl.multiple_of(i * cols, cols), cols)
+        values = second[:, span]
+        held[:, span] = jnp.maximum(values * scale + shift, 0.0).astype(held.dtype)
+        write(i).start()
+        return c
+
+    steps = sems.shape[0]
+    lax.fori_loop(0, steps, one, 0)
     mean1[...] = stats1[0:1, :]
     var1[...] = stats1[1:2, :]
     mean2[...] = stats2[0:1, :]
     var2[...] = stats2[1:2, :]
+    lax.fori_loop(0, steps, lambda i, c: (write(i).wait(), c)[1], 0)
 
 
 def units_of(block):
@@ -437,7 +482,8 @@
             pltpu.VMEM((wide, width), jnp.bfloat16),
             pltpu.VMEM((n, width), jnp.float32),
             pltpu.VMEM((n, width), jnp.float32),
-            pltpu.VMEM((total, depth), jnp.bfloat16),
+            pltpu.VMEM((total // 2, depth), jnp.bfloat16),
+            pltpu.VMEM((total, wide), jnp.bfloat16),
             pltpu.VMEM((2, width, 128), jnp.float32),
             pltpu.VMEM((8, wide), jnp.float32),
             pltpu.VMEM((n, 8, wide), jnp.float32),
@@ -482,7 +528,7 @@
         )
     )
     lanes = total // 128
-    steps = next(s for s in range(7, lanes + 1) if lanes % s == 0)
+    steps = next(s for s in range(14, lanes + 1) if lanes % s == 0)
     cols = total // steps
     output, mean1, var1, mean2, var2 = pl.pallas_call(
         functools.partial(finish_kernel, cols),
@@ -493,15 +539,9 @@
             jax.ShapeDtypeStruct((1, width), jnp.float32),
             jax.ShapeDtypeStruct((1, width), jnp.float32),
         ),
-        grid=(steps,),
         in_specs=[vmem, vmem, vmem],
-        out_specs=(
-            pl.BlockSpec((width, cols), lambda i: (0, i)),
-            pl.BlockSpec((1, wide), lambda i: (0, 0)),
-            pl.BlockSpec((1, wide), lambda i: (0, 0)),
-            pl.BlockSpec((1, width), lambda i: (0, 0)),
-            pl.BlockSpec((1, width), lambda i: (0, 0)),
-        ),
+        out_specs=(hbm, vmem, vmem, vmem, vmem),
+        scratch_shapes=[pltpu.VMEM((width, total), jnp.bfloat16), dma((steps,))],
         compiler_params=pltpu.CompilerParams(vmem_limit_bytes=VMEM_ASKED // 2),
         name="second_norm",
     )(*(pltpu.with_memory_space_constraint(x, pltpu.VMEM) for x in (stats1, stats2, second)))

time: 73.7 us -> 72.5 us (0.984)
  Pallas kernels: 73 us -> 71.8 us
    pallas_call x1, Pallas kernels: 5.14 us -> 4.3 us  [gather_shards(): pl.pallas_call(functools.partial(finish_kernel, cols), out_shape=(jax.Sha...]
where the time goes in v3:
time: 72.5 us; the launch traced here: 72.4 us
  Pallas kernels  71.8 us (99%)
    pallas_call x1, Pallas kernels, gather_shards(): pl.pallas_call(functools.partial(gather_kernel, (n, ns, units, unit, tile...  67.4 us
    pallas_call x1, Pallas kernels, gather_shards(): pl.pallas_call(functools.partial(finish_kernel, cols), out_shape=(jax.Sha...  4.3 us

profile of v3, /device:TPU:0, one launch (start us, length us, event | category | flops | bytes accessed | tf_op | source)
XLA Modules:
  0.0 72.4 jit_solution(7512401268090510801)
XLA Ops:
  0.6 67.4 %gather_convs.1 = (f32[128,25088]{1,0:T(8,128)S(1)}, f32[8,512]{1,0:T(8,128)S(1)}, f32[8,128]{1,0:T(8,128)S(1)}) custom-call(s32[1,32]{1,0:T(1,128)} %tissue_in.1, bf16[3136,256]{1,0:T(8,128)(2,1)} %bitcast.11, bf16[256,512]{1,0:T(8,128)(2,1)} %w1_in.1, f32[1,512]{1,0:T(1,128)} %bitcast.14, f32[1,512]{1,0:T(1,128)} %bitcast.15, bf16[512,128]{1,0:T(8,128)(2,1)} %w2_in.1, ...), custom_call_target="tpu_custom_call" | custom-call | flops 9865003008 | bytes 1605632 | tf_op jit(solution)/shard_map/gather_convs/pallas_call | solution.py:468
  68.1 4.3 %second_norm.1 = (bf16[128,25088]{1,0:T(8,128)(2,1)}, f32[1,512]{1,0:T(1,128)}, f32[1,512]{1,0:T(1,128)}, f32[1,128]{1,0:T(1,128)}, f32[1,128]{1,0:T(1,128)}) custom-call(f32[8,512]{1,0:T(8,128)S(1)} %get-tuple-element.13.stats1, f32[8,128]{1,0:T(8,128)S(1)} %get-tuple-element.14.stats2, f32[128,25088]{1,0:T(8,128)S(1)} %get-tuple-element.15.second), custom_call_target="tpu_custom_call" | custom-call | tf_op jit(solution)/shard_map/second_norm/pallas_call | solution.py:533

commit v4 on v3

--- a/solution.py
+++ b/solution.py
@@ -254,8 +254,9 @@
         return (other, me)
 
     copies = exchange(st1, me, n, st1_send, st1_recv, in_space)
-    lax.fori_loop(2, units, lambda k, c: (start_own(k), c)[1], 0)
+    start_own(2)
     collect(st1, copies, st1_recv, st1_send, in_space)
+    start_own(3)
     st2[sec] = jnp.sum(st1[...], axis=0)
     copies = exchange(st2, sec, ns, st2_send, st2_recv, in_section)
     collect(st2, copies, st2_recv, st2_send, in_section)
@@ -330,9 +331,24 @@
         lax.fori_loop(0, 2, one, 0)
 
     last = macros - 1
+    ahead = 4
+
+    def own_left(k):
+        for copy in own_copies(k):
+            copy.wait_send()
+
+    def from_b(k):
+        arrived(0, chip_b, k)
+        forward(k).start()
 
     def own_step(m, c):
+        @pl.when(m + ahead < units)
+        def _():
+            own_left(m)
+            start_own(m + ahead)
+
         each_unit(m, lambda k: activate(0, chip_o, k))
+        from_b(m)
 
         @pl.when(m > 0)
         def _():
@@ -341,14 +357,13 @@
         return c
 
     def side_step(m, c):
-        def from_b(k):
-            arrived(0, chip_b, k)
-            forward(k).start()
-
         def from_a(k):
             arrived(1, chip_a, k)
 
-        each_unit(m, from_b)
+        def later_b(k):
+            pl.when(k >= macros)(lambda: from_b(k))
+
+        each_unit(m, later_b)
         each_unit(m, from_a)
 
         def one(s, c):
@@ -386,6 +401,13 @@
         return c
 
     lax.fori_loop(0, macros, own_step, 0)
+
+    def rest(k, c):
+        own_left(k - ahead)
+        start_own(k)
+        return c
+
+    lax.fori_loop(macros + ahead, units, rest, 0)
     lax.fori_loop(0, macros, side_step, 0)
     lax.fori_loop(0, macros, last_step, 0)
     finish(3, chip_d, last)
@@ -398,8 +420,7 @@
     copies = exchange(st3, sec, ns, st3_send, st3_recv, in_section)
 
     def drain(k, c):
-        for copy in own_copies(k):
-            copy.wait_send()
+        pl.when(k + ahead >= units)(lambda: own_left(k))
         for group in range(4):
             relay(group, chip_o, core, k).wait_send()
         forward(k).wait_send()
@@ -445,7 +466,7 @@
 
 
 def units_of(block):
-    for units in range(3, block, 2):
+    for units in range(5, block, 2):
         unit = block // units
         if block % units == 0 and unit <= 512 and unit % 64 == 0:
             return units

time: 72.5 us -> 72.5 us (level)
  no operation moved by 1% of the time
where the time goes in v4:
time: 72.5 us; the launch traced here: 72.4 us
  Pallas kernels  71.8 us (99%)
    pallas_call x1, Pallas kernels, gather_shards(): pl.pallas_call(functools.partial(gather_kernel, (n, ns, units, unit, tile...  67.4 us
    pallas_call x1, Pallas kernels, gather_shards(): pl.pallas_call(functools.partial(finish_kernel, cols), out_shape=(jax.Sha...  4.3 us

profile of v4, /device:TPU:0, one launch (start us, length us, event | category | flops | bytes accessed | tf_op | source)
XLA Modules:
  0.0 72.4 jit_solution(17830238282497765088)
XLA Ops:
  0.6 67.4 %gather_convs.1 = (f32[128,25088]{1,0:T(8,128)S(1)}, f32[8,512]{1,0:T(8,128)S(1)}, f32[8,128]{1,0:T(8,128)S(1)}) custom-call(s32[1,32]{1,0:T(1,128)} %tissue_in.1, bf16[3136,256]{1,0:T(8,128)(2,1)} %bitcast.11, bf16[256,512]{1,0:T(8,128)(2,1)} %w1_in.1, f32[1,512]{1,0:T(1,128)} %bitcast.14, f32[1,512]{1,0:T(1,128)} %bitcast.15, bf16[512,128]{1,0:T(8,128)(2,1)} %w2_in.1, ...), custom_call_target="tpu_custom_call" | custom-call | flops 9865003008 | bytes 1605632 | tf_op jit(solution)/shard_map/gather_convs/pallas_call | solution.py:489
  68.1 4.3 %second_norm.1 = (bf16[128,25088]{1,0:T(8,128)(2,1)}, f32[1,512]{1,0:T(1,128)}, f32[1,512]{1,0:T(1,128)}, f32[1,128]{1,0:T(1,128)}, f32[1,128]{1,0:T(1,128)}) custom-call(f32[8,512]{1,0:T(8,128)S(1)} %get-tuple-element.13.stats1, f32[8,128]{1,0:T(8,128)S(1)} %get-tuple-element.14.stats2, f32[128,25088]{1,0:T(8,128)S(1)} %get-tuple-element.15.second), custom_call_target="tpu_custom_call" | custom-call | tf_op jit(solution)/shard_map/second_norm/pallas_call | solution.py:554

commit v5 on v3

--- a/solution.py
+++ b/solution.py
@@ -419,28 +419,41 @@
     stats2_ref[4:8, :] = jnp.zeros((4, width), jnp.float32)
 
 
-def finish_kernel(cols, stats1, stats2, second, out, mean1, var1, mean2, var2, held, sems):
+def finish_kernel(
+    cols, stats1, stats2, second, out, mean1, var1, mean2, var2,
+    held, rows1, rows2, sems, stat_sems,
+):
     size = stats2.shape[1]
-    scale = jnp.broadcast_to(stats2[2:3, :], (size, size)).T[:, 0:1]
-    shift = jnp.broadcast_to(stats2[3:4, :], (size, size)).T[:, 0:1]
+    scale = jnp.broadcast_to(stats2[2:3, :], (size, size)).T
+    shift = jnp.broadcast_to(stats2[3:4, :], (size, size)).T
+    for i in range(2):
+        rows1[i] = stats1[i:i + 1, :]
+        rows2[i] = stats2[i:i + 1, :]
+    small = [
+        pltpu.make_async_copy(src, dst, stat_sems.at[i])
+        for i, (src, dst) in enumerate(
+            ((rows1.at[0], mean1), (rows1.at[1], var1), (rows2.at[0], mean2), (rows2.at[1], var2))
+        )
+    ]
+    for copy in small:
+        copy.start()
 
     def write(i):
         span = pl.ds(pl.multiple_of(i * cols, cols), cols)
         return pltpu.make_async_copy(held.at[:, span], out.at[:, span], sems.at[i])
 
     def one(i, c):
-        span = pl.ds(pl.multiple_of(i * cols, cols), cols)
-        values = second[:, span]
-        held[:, span] = jnp.maximum(values * scale + shift, 0.0).astype(held.dtype)
+        for j in range(cols // size):
+            span = pl.ds(pl.multiple_of(i * cols + j * size, size), size)
+            values = second[:, span] * scale + shift
+            held[:, span] = jnp.maximum(values, 0.0).astype(held.dtype)
         write(i).start()
         return c
 
     steps = sems.shape[0]
     lax.fori_loop(0, steps, one, 0)
-    mean1[...] = stats1[0:1, :]
-    var1[...] = stats1[1:2, :]
-    mean2[...] = stats2[0:1, :]
-    var2[...] = stats2[1:2, :]
+    for copy in small:
+        copy.wait()
     lax.fori_loop(0, steps, lambda i, c: (write(i).wait(), c)[1], 0)
 
 
@@ -540,8 +553,14 @@
             jax.ShapeDtypeStruct((1, width), jnp.float32),
         ),
         in_specs=[vmem, vmem, vmem],
-        out_specs=(hbm, vmem, vmem, vmem, vmem),
-        scratch_shapes=[pltpu.VMEM((width, total), jnp.bfloat16), dma((steps,))],
+        out_specs=(hbm,) * 5,
+        scratch_shapes=[
+            pltpu.VMEM((width, total), jnp.bfloat16),
+            pltpu.VMEM((2, 1, wide), jnp.float32),
+            pltpu.VMEM((2, 1, width), jnp.float32),
+            dma((steps,)),
+            dma((4,)),
+        ],
         compiler_params=pltpu.CompilerParams(vmem_limit_bytes=VMEM_ASKED // 2),
         name="second_norm",
     )(*(pltpu.with_memory_space_constraint(x, pltpu.VMEM) for x in (stats1, stats2, second)))

time: 72.5 us -> 72 us (level)
  no operation moved by 1% of the time
where the time goes in v5:
time: 72 us; the launch traced here: 71.8 us
  Pallas kernels  71.2 us (99%)
    pallas_call x1, Pallas kernels, gather_shards(): pl.pallas_call(functools.partial(gather_kernel, (n, ns, units, unit, tile...  67.4 us
    pallas_call x1, Pallas kernels, gather_shards(): pl.pallas_call(functools.partial(finish_kernel, cols), out_shape=(jax.Sha...  3.72 us

profile of v5, /device:TPU:0, one launch (start us, length us, event | category | flops | bytes accessed | tf_op | source)
XLA Modules:
  0.0 71.8 jit_solution(855182774205918195)
XLA Ops:
  0.6 67.4 %gather_convs.1 = (f32[128,25088]{1,0:T(8,128)S(1)}, f32[8,512]{1,0:T(8,128)S(1)}, f32[8,128]{1,0:T(8,128)S(1)}) custom-call(s32[1,32]{1,0:T(1,128)} %tissue_in.1, bf16[3136,256]{1,0:T(8,128)(2,1)} %bitcast.11, bf16[256,512]{1,0:T(8,128)(2,1)} %w1_in.1, f32[1,512]{1,0:T(1,128)} %bitcast.14, f32[1,512]{1,0:T(1,128)} %bitcast.15, bf16[512,128]{1,0:T(8,128)(2,1)} %w2_in.1, ...), custom_call_target="tpu_custom_call" | custom-call | flops 9865003008 | bytes 1605632 | tf_op jit(solution)/shard_map/gather_convs/pallas_call | solution.py:481
  68.1 3.7 %second_norm.1 = (bf16[128,25088]{1,0:T(8,128)(2,1)}, f32[1,512]{1,0:T(1,128)}, f32[1,512]{1,0:T(1,128)}, f32[1,128]{1,0:T(1,128)}, f32[1,128]{1,0:T(1,128)}) custom-call(f32[8,512]{1,0:T(8,128)S(1)} %get-tuple-element.13.stats1, f32[8,128]{1,0:T(8,128)S(1)} %get-tuple-element.14.stats2, f32[128,25088]{1,0:T(8,128)S(1)} %get-tuple-element.15.second), custom_call_target="tpu_custom_call" | custom-call | tf_op jit(solution)/shard_map/second_norm/pallas_call | solution.py:546

commit v6 on v5

--- a/solution.py
+++ b/solution.py
@@ -379,16 +379,22 @@
 
         each_unit(m, from_d)
 
-        @pl.when(m > 0)
-        def _():
-            finish(3, chip_d, m - 1)
+        @pl.when(m < last)
+        def _():
+            compute(chip_d, m + macros * core)
+
+        each_unit(m, lambda k: relay(3, chip_d, 1 - core, k).wait_recv())
+
+        @pl.when(m < last)
+        def _():
+            compute(chip_d, m + macros * (1 - core))
 
         return c
 
     lax.fori_loop(0, macros, own_step, 0)
     lax.fori_loop(0, macros, side_step, 0)
     lax.fori_loop(0, macros, last_step, 0)
-    finish(3, chip_d, last)
+    compute(chip_d, last)
 
     width = w2.shape[1]
     mine = st3.at[sec]

time: 72 us -> 72 us (level)
  no operation moved by 1% of the time
where the time goes in v6:
time: 72 us; the launch traced here: 71.8 us
  Pallas kernels  71.2 us (99%)
    pallas_call x1, Pallas kernels, gather_shards(): pl.pallas_call(functools.partial(gather_kernel, (n, ns, units, unit, tile...  67.5 us
    pallas_call x1, Pallas kernels, gather_shards(): pl.pallas_call(functools.partial(finish_kernel, cols), out_shape=(jax.Sha...  3.72 us

profile of v6, /device:TPU:0, one launch (start us, length us, event | category | flops | bytes accessed | tf_op | source)
XLA Modules:
  0.0 71.8 jit_solution(6382732131022124216)
XLA Ops:
  0.6 67.5 %gather_convs.1 = (f32[128,25088]{1,0:T(8,128)S(1)}, f32[8,512]{1,0:T(8,128)S(1)}, f32[8,128]{1,0:T(8,128)S(1)}) custom-call(s32[1,32]{1,0:T(1,128)} %tissue_in.1, bf16[3136,256]{1,0:T(8,128)(2,1)} %bitcast.11, bf16[256,512]{1,0:T(8,128)(2,1)} %w1_in.1, f32[1,512]{1,0:T(1,128)} %bitcast.14, f32[1,512]{1,0:T(1,128)} %bitcast.15, bf16[512,128]{1,0:T(8,128)(2,1)} %w2_in.1, ...), custom_call_target="tpu_custom_call" | custom-call | flops 9865003008 | bytes 1605632 | tf_op jit(solution)/shard_map/gather_convs/pallas_call | solution.py:487
  68.1 3.7 %second_norm.1 = (bf16[128,25088]{1,0:T(8,128)(2,1)}, f32[1,512]{1,0:T(1,128)}, f32[1,512]{1,0:T(1,128)}, f32[1,128]{1,0:T(1,128)}, f32[1,128]{1,0:T(1,128)}) custom-call(f32[8,512]{1,0:T(8,128)S(1)} %get-tuple-element.13.stats1, f32[8,128]{1,0:T(8,128)S(1)} %get-tuple-element.14.stats2, f32[128,25088]{1,0:T(8,128)S(1)} %get-tuple-element.15.second), custom_call_target="tpu_custom_call" | custom-call | tf_op jit(solution)/shard_map/second_norm/pallas_call | solution.py:552
